TPU v7x, 1024 devices: a whole 8x8x8 slice. The times are simulated.
1024 devices in a mesh: gx: 16 (over z, core), gy: 64 (over x, y).
Axes of the slice: x: 8, y: 8, z: 8, core: 2. Of those that a mesh axis runs over, the one named last changes fastest.
Arguments:
- tokens: bfloat16 [512, 10240], P('gy', 'gx'), may hold values from -6 to 6
- gate_pre: bfloat16 [512, 40960], P('gx', 'gy'), may hold values from -6 to 6
- up_pre: bfloat16 [512, 40960], P('gx', 'gy'), may hold values from -6 to 6
- hidden_grad: bfloat16 [512, 40960], P('gx', 'gy'), may hold values from -5 to 5
- w_gate: bfloat16 [10240, 40960], P('gx', 'gy'), may hold values from -0.0625 to 0.0625
- w_up: bfloat16 [10240, 40960], P('gx', 'gy'), may hold values from -0.0625 to 0.0625
Outputs:
- input_grad: bfloat16 [512, 10240], P('gy', 'gx')
- gate_weight_grad: bfloat16 [10240, 40960], P('gx', 'gy')
- up_weight_grad: bfloat16 [10240, 40960], P('gx', 'gy')
All inputs are finite; a program needn't handle non-finite values.
Results may differ from a plain program's by a relative error of at most 0.0049.
Values may be sent and summed in bfloat16 or wider, within the bound.
A program may use at most 32 MiB of HBM per device.

v0:
```python
import jax
import jax.numpy as jnp
from jax import lax
from jax.sharding import PartitionSpec as P


def contract_last(left, right):
    return lax.dot_general(
        left, right, (((1,), (1,)), ((), ())), preferred_element_type=jnp.float32
    )


def contract_first(left, right):
    return lax.dot_general(
        left, right, (((0,), (0,)), ((), ())), preferred_element_type=jnp.float32
    )


def local(tokens, gate_pre, up_pre, hidden_grad, w_gate, w_up):
    gate_vals = gate_pre.astype(jnp.float32)
    up_vals = up_pre.astype(jnp.float32)
    grad_vals = hidden_grad.astype(jnp.float32)
    sig = jax.nn.sigmoid(gate_vals)
    gate_grad = (grad_vals * up_vals * sig * (1.0 + gate_vals * (1.0 - sig))).astype(jnp.bfloat16)
    up_grad = (grad_vals * gate_vals * sig).astype(jnp.bfloat16)
    gate_all = lax.all_gather(gate_grad, "gx", axis=0, tiled=True)
    up_all = lax.all_gather(up_grad, "gx", axis=0, tiled=True)
    all_tokens = lax.all_gather(tokens, "gy", axis=0, tiled=True)
    input_grad = lax.psum_scatter(
        contract_last(gate_all, w_gate) + contract_last(up_all, w_up),
        "gy",
        scatter_dimension=0,
        tiled=True,
    ).astype(jnp.bfloat16)
    gate_weight_grad = contract_first(all_tokens, gate_all).astype(jnp.bfloat16)
    up_weight_grad = contract_first(all_tokens, up_all).astype(jnp.bfloat16)
    return (input_grad, gate_weight_grad, up_weight_grad)


def solution(mesh):
    return jax.shard_map(
        local,
        mesh=mesh,
        in_specs=(
            P("gy", "gx"),
            P("gx", "gy"),
            P("gx", "gy"),
            P("gx", "gy"),
            P("gx", "gy"),
            P("gx", "gy"),
        ),
        out_specs=(P("gy", "gx"), P("gx", "gy"), P("gx", "gy")),
        check_vma=False,
    )
```

profile of v0, /device:TPU:2, one launch (start us, length us, event | category | flops | bytes accessed | tf_op | source)
XLA Modules:
  0.0 399.5 jit_solution(14824368514449462291)
XLA Ops:
  0.6 0.0 copy-start
  0.6 0.9 fusion.10
  1.6 31.3 %all_gather.9 = bf16[512,640]{1,0:T(8,128)(2,1)S(1)} all-gather(bf16[32,640]{1,0:T(8,128)(2,1)S(1)} %get-tuple-element.10), channel_id=1, replica_groups=mesh['gx'=16,'gy'=64] {'gx'}, dimensions={0}, use_global_device_ids=true | all-gather | bytes 696320 | tf_op jit(solution)/shard_map/all_gather | solution.py:26
  32.9 0.0 copy-done
  32.9 0.0 copy-start.1
  32.9 0.8 fusion.11
  33.7 16.3 %all_gather.10 = bf16[512,640]{1,0:T(8,128)(2,1)S(1)} all-gather(bf16[32,640]{1,0:T(8,128)(2,1)S(1)} %get-tuple-element.9), channel_id=1, replica_groups=mesh['gx'=16,'gy'=64] {'gx'}, dimensions={0}, use_global_device_ids=true | all-gather | bytes 696320 | tf_op jit(solution)/shard_map/all_gather | solution.py:27
  50.0 0.0 copy-done.1
  50.0 0.8 convolution_add_fusion
  50.8 0.0 copy-start.4
  50.8 281.3 %all-reduce.2 = bf16[512,640]{1,0:T(8,128)(2,1)} all-reduce(f32[512,640]{1,0:T(8,128)S(1)} %convolution_add_fusion), channel_id=2, replica_groups=mesh['gx'=16,'gy'=64] {'gy'}, use_global_device_ids=true, to_apply=%region_0.0.clone | all-reduce | flops 327680 | bytes 1966080
  332.1 1.3 dynamic-slice
  334.0 1.3 dynamic-slice_convert_fusion
  335.3 0.0 copy-done.4
  335.3 59.3 %all_gather.11 = bf16[512,640]{1,0:T(8,128)(2,1)S(1)} all-gather(bf16[8,640]{1,0:T(8,128)(2,1)S(1)} %copy-done.4), channel_id=1, replica_groups=mesh['gx'=16,'gy'=64] {'gy'}, dimensions={0}, use_global_device_ids=true | all-gather | bytes 665600 | tf_op jit(solution)/shard_map/all_gather | solution.py:28
  394.6 0.0 copy-start.2
  394.6 0.8 copy-done.2
  395.4 0.7 fusion
  396.1 0.0 copy-start.3
  396.1 1.3 copy.11
  397.5 0.0 copy-done.3
  397.5 0.7 fusion.1
  398.2 1.3 copy.12
Async XLA Ops:
  0.6 32.3 %copy-start = (bf16[640,640]{1,0:T(8,128)(2,1)S(1)}, bf16[640,640]{1,0:T(8,128)(2,1)}, u32[]{:S(2)}) copy-start(bf16[640,640]{1,0:T(8,128)(2,1)} %param.10) | copy-start | bytes 2457604
  32.9 17.1 %copy-start.1 = (bf16[640,640]{1,0:T(8,128)(2,1)S(1)}, bf16[640,640]{1,0:T(8,128)(2,1)}, u32[]{:S(2)}) copy-start(bf16[640,640]{1,0:T(8,128)(2,1)} %param.11) | copy-start | bytes 2457604
  50.8 284.5 %copy-start.4 = (bf16[8,640]{1,0:T(8,128)(2,1)S(1)}, bf16[8,640]{1,0:T(8,128)(2,1)}, u32[]{:S(2)}) copy-start(bf16[8,640]{1,0:T(8,128)(2,1)} %param.6) | copy-start | bytes 30724
  394.6 0.8 copy-start.2
  396.1 1.3 copy-start.3
where the time goes:
time: 400 us; the launch traced here: 399 us
  blocking collectives  388 us (97%)
  local copies, waits for them, and re-layouts  6.05 us (2%)
    unnamed x1, blocking collectives  281 us
    all_gather x1, blocking collectives, local(): all_tokens = lax.all_gather(tokens, 'gy', axis=0, tiled=True)  59.3 us
    all_gather x1, blocking collectives, local(): gate_all = lax.all_gather(gate_grad, 'gx', axis=0, tiled=True)  31.3 us
    all_gather x1, blocking collectives, local(): up_all = lax.all_gather(up_grad, 'gx', axis=0, tiled=True)  16.3 us

commit v1 on v0

v1 whole, which is shorter than its diff:
```python
import functools

import jax
import jax.numpy as jnp
from jax import lax
from jax.experimental import pallas as pl
from jax.experimental.pallas import tpu as pltpu
from jax.sharding import PartitionSpec as P

MESH = pl.DeviceIdType.MESH
F32 = jnp.float32
BF16 = jnp.bfloat16


def slot_of(delta, n):
    if delta == 0:
        return 0
    if delta <= n // 2 - 1:
        return 2 * delta - 1
    if delta == n // 2:
        return n - 1
    return 2 * (n - delta)


def slot_dynamic(delta, n):
    near = jnp.where(delta == n // 2, n - 1, 2 * delta - 1)
    far = 2 * (n - delta)
    return jnp.where(delta == 0, 0, jnp.where(delta <= n // 2, near, far))


def delta_of(slot, n):
    return next(d for d in range(n) if slot_of(d, n) == slot)


def groups_of(n):
    groups = [(0, 3)]
    for step in range(2, n // 2):
        groups.append((2 * step - 1, 2 * step + 1))
    groups.append((n - 1, n))
    return groups


def kernel(n, rows, *refs):
    (
        tok_hbm, gate_hbm, up_hbm, grad_hbm, wg_hbm, wu_hbm,
        out_ref, dwg_hbm, dwu_hbm,
        gate_v, up_v, grad_v, wg, wu, gu, tok, tok2, dwg, dwu, sums, part2,
        *more,
    ) = refs
    groups = groups_of(n)
    ng = len(groups)
    parts = more[:ng]
    recvs = more[ng:2 * ng]
    (
        load_sem, store_sem, z_send, z_recv, sib_send, sib_recv,
        t1_send, t1_recv, t2_send, t2_recv, s1_send, s1_recv, s2_send, s2_recv,
    ) = more[2 * ng:]
    half = n // 2
    gx = lax.axis_index("gx")
    gy = lax.axis_index("gy")
    z, c = gx // 2, gx % 2
    x, y = gy // n, gy % n
    first = c == 0
    a = jnp.where(first, x, y)
    b = jnp.where(first, y, x)

    def at_ab(a_at, b_at):
        return (gx, jnp.where(first, a_at * n + b_at, b_at * n + a_at))

    def at_z(z_at):
        return (z_at * 2 + c, gy)

    sibling = (gx + 1 - 2 * c, gy)
    up_z = at_z((z + 1) % n)
    down_z = at_z((z + n - 1) % n)
    next_a = at_ab((a + 1) % n, b)
    prev_a = at_ab((a + n - 1) % n, b)

    def remote(src, dst, send, recv, to):
        copy = pltpu.make_async_remote_copy(
            src_ref=src, dst_ref=dst, send_sem=send, recv_sem=recv,
            device_id=to, device_id_type=MESH,
        )
        copy.start()
        return copy

    loads = [
        pltpu.make_async_copy(src, dst, load_sem.at[i])
        for i, (src, dst) in enumerate(
            (
                (gate_hbm, gate_v), (up_hbm, up_v), (grad_hbm, grad_v),
                (tok_hbm, tok.at[a, b]),
                (wg_hbm, wg), (wu_hbm, wu),
            )
        )
    ]
    for load in loads:
        load.start()

    barrier = pltpu.get_barrier_semaphore()

    def greet(to):
        pl.semaphore_signal(barrier, inc=1, device_id=to, device_id_type=MESH)

    greet(sibling)
    greet(up_z)
    greet(down_z)
    greet(next_a)
    greet(prev_a)
    for k in range(1, n):
        greet(at_ab(a, (b + k) % n))
    for j in range(n):
        @pl.when(jnp.logical_not((a == j) & (b == y)))
        def _():
            greet(at_ab(j, y))

    for load in loads[:3]:
        load.wait()
    gate = gate_v[...].astype(F32)
    up = up_v[...].astype(F32)
    grad = grad_v[...].astype(F32)
    sig = 1.0 / (1.0 + jnp.exp(-gate))
    gu[0, 0, c] = (grad * up * sig * (1.0 + gate * (1.0 - sig))).astype(BF16)
    gu[1, 0, c] = (grad * gate * sig).astype(BF16)

    self_dest = jnp.where(b == y, 1, 0)
    pl.semaphore_wait(barrier, 5 + (n - 1) + n - self_dest)

    pending = []

    def ring_slot(direction, step):
        return slot_of((n - step) % n if direction == 0 else step, n)

    def ring_send(direction, step, chunk):
        pending.append(
            remote(
                gu.at[chunk, ring_slot(direction, step - 1), c],
                gu.at[chunk, ring_slot(direction, step), c],
                z_send.at[direction, step - 1, chunk],
                z_recv.at[direction, step - 1, chunk],
                up_z if direction == 0 else down_z,
            )
        )

    def ring_wait(direction, step, chunk):
        slot = ring_slot(direction, step)
        pltpu.make_async_remote_copy(
            src_ref=gu.at[chunk, slot, c], dst_ref=gu.at[chunk, slot, c],
            send_sem=z_send.at[direction, step - 1, chunk],
            recv_sem=z_recv.at[direction, step - 1, chunk],
            device_id=sibling, device_id_type=MESH,
        ).wait_recv()

    def travels(direction, step, chunk):
        return step < half or (step == half and chunk == direction)

    def sib_share(slot, chunk):
        pending.append(
            remote(
                gu.at[chunk, slot, c], gu.at[chunk, slot, c],
                sib_send.at[slot, chunk], sib_recv.at[slot, chunk], sibling,
            )
        )

    def sib_wait(slot, chunk):
        pltpu.make_async_remote_copy(
            src_ref=gu.at[chunk, slot, 1 - c], dst_ref=gu.at[chunk, slot, 1 - c],
            send_sem=sib_send.at[slot, chunk], recv_sem=sib_recv.at[slot, chunk],
            device_id=sibling, device_id_type=MESH,
        ).wait_recv()

    for chunk in range(2):
        for direction in range(2):
            ring_send(direction, 1, chunk)
    for chunk in range(2):
        sib_share(0, chunk)

    loads[3].wait()
    for k in range(1, n):
        pending.append(
            remote(
                tok.at[a, b], tok.at[a, b], t1_send.at[k - 1], t1_recv.at[k - 1],
                at_ab(a, (b + k) % n),
            )
        )

    def tok_send(direction, step):
        block = (a - (step - 1) + n) % n if direction == 0 else (a + step - 1) % n
        lo, hi = tok_part(direction, step)
        pending.append(
            remote(
                tok.at[block, lo:hi], tok.at[block, lo:hi],
                t2_send.at[direction, step - 1], t2_recv.at[direction, step - 1],
                next_a if direction == 0 else prev_a,
            )
        )

    def tok_part(direction, step):
        if step < half:
            return 0, n
        return (0, half) if direction == 0 else (half, n)

    def tok_wait(direction, step):
        block = (a - step + n) % n if direction == 0 else (a + step) % n
        lo, hi = tok_part(direction, step)
        pltpu.make_async_remote_copy(
            src_ref=tok.at[block, lo:hi], dst_ref=tok.at[block, lo:hi],
            send_sem=t2_send.at[direction, step - 1],
            recv_sem=t2_recv.at[direction, step - 1],
            device_id=sibling, device_id_type=MESH,
        ).wait_recv()

    def tok_first():
        for k in range(1, n):
            pltpu.make_async_remote_copy(
                src_ref=tok.at[a, b], dst_ref=tok.at[a, (b + n - k) % n],
                send_sem=t1_send.at[k - 1], recv_sem=t1_recv.at[k - 1],
                device_id=sibling, device_id_type=MESH,
            ).wait_recv()
        for direction in range(2):
            tok_send(direction, 1)

    def multiply(index):
        lo, hi = groups[index]
        m = (hi - lo) * 2 * rows
        left_g = gu[0, lo:hi].reshape(m, gu.shape[-1])
        left_u = gu[1, lo:hi].reshape(m, gu.shape[-1])
        dims = (((1,), (1,)), ((), ()))
        total = lax.dot_general(left_g, wg[...], dims, preferred_element_type=F32)
        total += lax.dot_general(left_u, wu[...], dims, preferred_element_type=F32)
        per = 2 * rows // n
        for i in range(hi - lo):
            parts[index][:, i] = (
                total[i * 2 * rows:(i + 1) * 2 * rows]
                .reshape(n, per, total.shape[-1]).astype(BF16)
            )
        for k in range(1, n):
            to = (b + k) % n
            pending.append(
                remote(
                    parts[index].at[to], recvs[index].at[k - 1],
                    s1_send.at[index, k - 1], s1_recv.at[index, k - 1], at_ab(a, to),
                )
            )

    def reduce_first(index):
        lo, hi = groups[index]
        for k in range(1, n):
            pltpu.make_async_remote_copy(
                src_ref=recvs[index].at[k - 1], dst_ref=recvs[index].at[k - 1],
                send_sem=s1_send.at[index, k - 1], recv_sem=s1_recv.at[index, k - 1],
                device_id=sibling, device_id_type=MESH,
            ).wait_recv()
        total = parts[index][b].astype(F32)
        for k in range(1, n):
            total += recvs[index][k - 1].astype(F32)
        sums[lo:hi] = total.astype(BF16)
        for slot in range(lo, hi):
            owner_x = (z + delta_of(slot, n)) % n
            mine = (owner_x == x) & (b == y)

            @pl.when(mine)
            def _():
                pltpu.make_async_copy(
                    sums.at[slot], part2.at[a], s2_recv.at[a]
                ).start()

            @pl.when(jnp.logical_not(mine))
            def _():
                remote(
                    sums.at[slot], part2.at[a], s2_send.at[slot], s2_recv.at[a],
                    (gx, owner_x * n + b),
                )

    def reduce_sent(slot):
        owner_x = (z + delta_of(slot, n)) % n
        mine = (owner_x == x) & (b == y)

        @pl.when(jnp.logical_not(mine))
        def _():
            pltpu.make_async_remote_copy(
                src_ref=sums.at[slot], dst_ref=part2.at[a],
                send_sem=s2_send.at[slot], recv_sem=s2_recv.at[a],
                device_id=sibling, device_id_type=MESH,
            ).wait_send()

    def weights(chunk, result, to, sem):
        right = gu[chunk].reshape(n * 2 * rows, gu.shape[-1])
        result[...] = lax.dot_general(
            tok2[...], right, (((0,), (0,)), ((), ())), preferred_element_type=F32
        ).astype(BF16)
        store = pltpu.make_async_copy(result, to, sem)
        store.start()
        return store

    tok_first()
    for step in range(1, half + 1):
        for chunk in range(2):
            for direction in range(2):
                if not travels(direction, step, chunk):
                    continue
                ring_wait(direction, step, chunk)
                if travels(direction, step + 1, chunk):
                    ring_send(direction, step + 1, chunk)
                sib_share(ring_slot(direction, step), chunk)
        for direction in range(2):
            tok_wait(direction, step)
            if step < half:
                tok_send(direction, step + 1)
        if step == 1:
            for chunk in range(2):
                sib_wait(0, chunk)
            loads[4].wait()
            loads[5].wait()
        for chunk in range(2):
            for slot in sorted({ring_slot(0, step), ring_slot(1, step)}):
                sib_wait(slot, chunk)
        multiply(step - 1)
        if step >= 2:
            reduce_first(step - 2)

    for slot in range(n):
        block = (z + delta_of(slot, n)) % n
        for pair in range(n // 2):
            two = []
            for at in (2 * pair, 2 * pair + 1):
                i = jnp.where(first, block, at)
                j = jnp.where(first, at, block)
                two.append(tok[i, j].astype(F32))
            per = tok.shape[2]
            start = (slot * n + 2 * pair) * per
            tok2[start:start + 2 * per] = jnp.concatenate(two, axis=0).astype(BF16)
    store_g = weights(0, dwg, dwg_hbm, store_sem.at[0])
    reduce_first(ng - 1)
    store_u = weights(1, dwu, dwu_hbm, store_sem.at[1])

    for j in range(n):
        pltpu.make_async_copy(sums.at[0], part2.at[j], s2_recv.at[j]).wait()
    total = part2[0].astype(F32)
    for j in range(1, n):
        total += part2[j].astype(F32)
    out_ref[...] = total.astype(BF16)
    store_g.wait()
    store_u.wait()
    for copy in pending:
        copy.wait_send()
    for slot in range(n):
        reduce_sent(slot)


def solution(mesh):
    n = mesh.shape["gx"] // 2

    def local(tokens, gate_pre, up_pre, hidden_grad, w_gate, w_up):
        per, d = tokens.shape
        rows, ff = gate_pre.shape
        groups = groups_of(n)
        ng = len(groups)
        any_spec = pl.BlockSpec(memory_space=pl.ANY)
        dma = pltpu.SemaphoreType.DMA
        half = n // 2
        scratch = [
            pltpu.VMEM((rows, ff), BF16),
            pltpu.VMEM((rows, ff), BF16),
            pltpu.VMEM((rows, ff), BF16),
            pltpu.VMEM((d, ff), BF16),
            pltpu.VMEM((d, ff), BF16),
            pltpu.VMEM((2, n, 2, rows, ff), BF16),
            pltpu.VMEM((n, n, per, d), BF16),
            pltpu.VMEM((n * n * per, d), BF16),
            pltpu.VMEM((d, ff), BF16),
            pltpu.VMEM((d, ff), BF16),
            pltpu.VMEM((n, per, d), BF16),
            pltpu.VMEM((n, per, d), BF16),
        ]
        scratch += [pltpu.VMEM((n, hi - lo, per, d), BF16) for lo, hi in groups]
        scratch += [pltpu.VMEM((n - 1, hi - lo, per, d), BF16) for lo, hi in groups]
        scratch += [
            dma((6,)), dma((2,)),
            dma((2, half, 2)), dma((2, half, 2)),
            dma((n, 2)), dma((n, 2)),
            dma((n - 1,)), dma((n - 1,)),
            dma((2, half)), dma((2, half)),
            dma((ng, n - 1)), dma((ng, n - 1)),
            dma((n,)), dma((n,)),
        ]
        return pl.pallas_call(
            functools.partial(kernel, n, rows),
            out_shape=(
                jax.ShapeDtypeStruct((per, d), BF16),
                jax.ShapeDtypeStruct((d, ff), BF16),
                jax.ShapeDtypeStruct((d, ff), BF16),
            ),
            in_specs=[any_spec] * 6,
            out_specs=(pl.BlockSpec(memory_space=pltpu.VMEM), any_spec, any_spec),
            scratch_shapes=scratch,
            compiler_params=pltpu.CompilerParams(
                collective_id=0, has_side_effects=True,
                vmem_limit_bytes=48 * 1024 * 1024,
            ),
            cost_estimate=pl.CostEstimate(
                flops=8 * n * n * per * d * ff, bytes_accessed=8 * d * ff,
                transcendentals=rows * ff,
            ),
        )(tokens, gate_pre, up_pre, hidden_grad, w_gate, w_up)

    return jax.shard_map(
        local,
        mesh=mesh,
        in_specs=(
            P("gy", "gx"),
            P("gx", "gy"),
            P("gx", "gy"),
            P("gx", "gy"),
            P("gx", "gy"),
            P("gx", "gy"),
        ),
        out_specs=(P("gy", "gx"), P("gx", "gy"), P("gx", "gy")),
        check_vma=False,
    )
```

time: 400 us -> 63.9 us (0.16)
  the two profiles are of different devices: /device:TPU:2 before, /device:TPU:9 now
where the time goes in v1:
time: 63.9 us; the launch traced here: 63.4 us
  Pallas kernels  55.1 us (86%)
  local copies, waits for them, and re-layouts  7.7 us (12%)
  between operations  0.65 us (1%)
    pallas_call x1, Pallas kernels, local(): pl.pallas_call(functools.partial(kernel, n, rows), out_shape=(jax.ShapeDt...  55.1 us
    unnamed x15, local copies, waits for them, and re-layouts  7.7 us

profile of v1, /device:TPU:9, one launch (start us, length us, event | category | flops | bytes accessed | tf_op | source)
XLA Modules:
  0.0 63.4 jit_solution(9217581779325922163)
XLA Ops:
  0.6 0.0 copy-start
  0.6 1.1 %copy-done = bf16[640,640]{1,0:T(8,128)(2,1)S(1)} copy-done((bf16[640,640]{1,0:T(8,128)(2,1)S(1)}, bf16[640,640]{1,0:T(8,128)(2,1)}, u32[]{:S(2)}) %copy-start) | copy-done | bytes 819224
  1.8 0.0 copy-start.1
  1.8 1.1 %copy-done.1 = bf16[640,640]{1,0:T(8,128)(2,1)S(1)} copy-done((bf16[640,640]{1,0:T(8,128)(2,1)S(1)}, bf16[640,640]{1,0:T(8,128)(2,1)}, u32[]{:S(2)}) %copy-start.1) | copy-done | bytes 819224
  2.9 0.0 copy-start.2
  2.9 0.8 %copy-done.2 = bf16[32,640]{1,0:T(8,128)(2,1)S(1)} copy-done((bf16[32,640]{1,0:T(8,128)(2,1)S(1)}, bf16[32,640]{1,0:T(8,128)(2,1)}, u32[]{:S(2)}) %copy-start.2) | copy-done | bytes 40984
  3.7 0.0 copy-start.3
  3.7 0.8 %copy-done.3 = bf16[32,640]{1,0:T(8,128)(2,1)S(1)} copy-done((bf16[32,640]{1,0:T(8,128)(2,1)S(1)}, bf16[32,640]{1,0:T(8,128)(2,1)}, u32[]{:S(2)}) %copy-start.3) | copy-done | bytes 40984
  4.5 0.0 copy-start.4
  4.5 0.8 %copy-done.4 = bf16[32,640]{1,0:T(8,128)(2,1)S(1)} copy-done((bf16[32,640]{1,0:T(8,128)(2,1)S(1)}, bf16[32,640]{1,0:T(8,128)(2,1)}, u32[]{:S(2)}) %copy-start.4) | copy-done | bytes 40984
  5.3 0.0 copy-start.5
  5.3 0.7 %copy-done.5 = bf16[8,640]{1,0:T(8,128)(2,1)S(1)} copy-done((bf16[8,640]{1,0:T(8,128)(2,1)S(1)}, bf16[8,640]{1,0:T(8,128)(2,1)}, u32[]{:S(2)}) %copy-start.5) | copy-done | bytes 10264
  6.0 55.1 %shard_map.85 = (bf16[8,640]{1,0:T(8,128)(2,1)S(1)}, bf16[640,640]{1,0:T(8,128)(2,1)S(1)}, bf16[640,640]{1,0:T(8,128)(2,1)S(1)}) custom-call(bf16[8,640]{1,0:T(8,128)(2,1)S(1)} %copy-done.5, bf16[32,640]{1,0:T(8,128)(2,1)S(1)} %copy-done.2, bf16[32,640]{1,0:T(8,128)(2,1)S(1)} %copy-done.3, bf16[32,640]{1,0:T(8,128)(2,1)S(1)} %copy-done.4, ...), custom_call_target="tpu_custom_call" | custom-call | flops 1677721600 | bytes 3276800 | tf_op jit(solution)/shard_map/pallas_call | solution.py:387
  61.1 0.6 copy.12
  61.7 0.9 %copy.13 = bf16[640,640]{1,0:T(8,128)(2,1)} copy(bf16[640,640]{1,0:T(8,128)(2,1)S(1)} %get-tuple-element.7) | data formatting | bytes 1638400
  62.6 0.9 %copy.14 = bf16[640,640]{1,0:T(8,128)(2,1)} copy(bf16[640,640]{1,0:T(8,128)(2,1)S(1)} %get-tuple-element.8) | data formatting | bytes 1638400
Async XLA Ops:
  0.6 1.1 %copy-start = (bf16[640,640]{1,0:T(8,128)(2,1)S(1)}, bf16[640,640]{1,0:T(8,128)(2,1)}, u32[]{:S(2)}) copy-start(bf16[640,640]{1,0:T(8,128)(2,1)} %refs_4_.1) | copy-start | bytes 2457604
  1.8 1.1 %copy-start.1 = (bf16[640,640]{1,0:T(8,128)(2,1)S(1)}, bf16[640,640]{1,0:T(8,128)(2,1)}, u32[]{:S(2)}) copy-start(bf16[640,640]{1,0:T(8,128)(2,1)} %refs_5_.1) | copy-start | bytes 2457604
  2.9 0.8 %copy-start.2 = (bf16[32,640]{1,0:T(8,128)(2,1)S(1)}, bf16[32,640]{1,0:T(8,128)(2,1)}, u32[]{:S(2)}) copy-start(bf16[32,640]{1,0:T(8,128)(2,1)} %refs_1_.1) | copy-start | bytes 122884
  3.7 0.8 %copy-start.3 = (bf16[32,640]{1,0:T(8,128)(2,1)S(1)}, bf16[32,640]{1,0:T(8,128)(2,1)}, u32[]{:S(2)}) copy-start(bf16[32,640]{1,0:T(8,128)(2,1)} %refs_2_.1) | copy-start | bytes 122884
  4.5 0.8 %copy-start.4 = (bf16[32,640]{1,0:T(8,128)(2,1)S(1)}, bf16[32,640]{1,0:T(8,128)(2,1)}, u32[]{:S(2)}) copy-start(bf16[32,640]{1,0:T(8,128)(2,1)} %refs_3_.1) | copy-start | bytes 122884
  5.3 0.7 %copy-start.5 = (bf16[8,640]{1,0:T(8,128)(2,1)S(1)}, bf16[8,640]{1,0:T(8,128)(2,1)}, u32[]{:S(2)}) copy-start(bf16[8,640]{1,0:T(8,128)(2,1)} %refs_0_.1) | copy-start | bytes 30724

commit v2 on v0

v2 whole, which is shorter than its diff:
```python
import functools

import jax
import jax.numpy as jnp
from jax import lax
from jax.experimental import pallas as pl
from jax.experimental.pallas import tpu as pltpu
from jax.sharding import PartitionSpec as P

MESH = pl.DeviceIdType.MESH
F32 = jnp.float32
BF16 = jnp.bfloat16
VMEM_MIB = 60


ORDER = (0, 2, 6, 1, 7, 3, 5, 4)
SLOT = {delta: slot for slot, delta in enumerate(ORDER)}
GROUPS = ((0, 1), (1, 3), (3, 5), (5, 8))
N = 8


def kernel(rows, *refs):
    (
        tok_hbm, gate_hbm, up_hbm, grad_hbm, wg_hbm, wu_hbm,
        out_ref, dwg_hbm, dwu_hbm,
        gate_v, up_v, grad_v, wg, wu, gu, tok, tok2, dwg, dwu, sums, part2,
        *more,
    ) = refs
    n = N
    ng = len(GROUPS)
    parts = more[:ng]
    recvs = more[ng:2 * ng]
    (
        load_sem, store_sem, z_send, z_recv, sib_send, sib_recv,
        t1_send, t1_recv, t2_send, t2_recv, s1_send, s1_recv, s2_send, s2_recv,
        near_sem,
    ) = more[2 * ng:]
    gx = lax.axis_index("gx")
    gy = lax.axis_index("gy")
    z, c = gx // 2, gx % 2
    x, y = gy // n, gy % n

    def at_z(step):
        return (((z + step + n) % n) * 2 + c, gy)

    def at_x(step):
        return (gx, ((x + step + n) % n) * n + y)

    def at_y(step):
        return (gx, x * n + (y + step + n) % n)

    sibling = (gx + 1 - 2 * c, gy)

    def signal(sem, to):
        pl.semaphore_signal(sem, inc=1, device_id=to, device_id_type=MESH)

    def copy_of(src, dst, send, recv, to):
        return pltpu.make_async_remote_copy(
            src_ref=src, dst_ref=dst, send_sem=send, recv_sem=recv,
            device_id=to, device_id_type=MESH,
        )

    pending = []

    def remote(*args):
        copy = copy_of(*args)
        copy.start()
        pending.append(copy)

    loads = [
        pltpu.make_async_copy(src, dst, load_sem.at[i])
        for i, (src, dst) in enumerate(
            (
                (gate_hbm, gate_v), (up_hbm, up_v), (grad_hbm, grad_v),
                (tok_hbm, tok.at[x, y]), (wg_hbm, wg), (wu_hbm, wu),
            )
        )
    ]
    for load in loads:
        load.start()

    barrier = pltpu.get_barrier_semaphore()
    near = (1, -1, 2, -2)
    for step in near:
        signal(barrier, at_z(step))
    signal(barrier, sibling)
    for step in near:
        signal(barrier, at_x(step))
        signal(barrier, at_y(step))

    for load in loads[:3]:
        load.wait()
    gate = gate_v[...].astype(F32)
    up = up_v[...].astype(F32)
    grad = grad_v[...].astype(F32)
    sig = 1.0 / (1.0 + jnp.exp(-gate))
    gu[0, 0, c] = (grad * up * sig * (1.0 + gate * (1.0 - sig))).astype(BF16)
    gu[1, 0, c] = (grad * gate * sig).astype(BF16)

    pl.semaphore_wait(barrier, 13)

    def z_send_on(held, via, chunk):
        delta = (held + via) % n
        remote(
            gu.at[chunk, SLOT[held % n], c], gu.at[chunk, SLOT[delta], c],
            z_send.at[SLOT[delta], chunk], z_recv.at[SLOT[delta], chunk],
            at_z(-via),
        )

    def z_wait(delta, chunk):
        ref = gu.at[chunk, SLOT[delta % n], c]
        copy_of(
            ref, ref, z_send.at[SLOT[delta % n], chunk],
            z_recv.at[SLOT[delta % n], chunk], sibling,
        ).wait_recv()

    def sib_share(delta, chunk):
        slot = SLOT[delta % n]
        ref = gu.at[chunk, slot, c]
        remote(ref, ref, sib_send.at[slot, chunk], sib_recv.at[slot, chunk], sibling)

    def sib_wait(delta, chunk):
        slot = SLOT[delta % n]
        ref = gu.at[chunk, slot, 1 - c]
        copy_of(
            ref, ref, sib_send.at[slot, chunk], sib_recv.at[slot, chunk], sibling
        ).wait_recv()

    for chunk in range(2):
        for via in (2, -2):
            z_send_on(0, via, chunk)
    for chunk in range(2):
        sib_share(0, chunk)
    for chunk in range(2):
        for via in (1, -1):
            z_send_on(0, via, chunk)

    for step in (2, -2):
        signal(near_sem, at_x(step))
        signal(near_sem, at_y(step))
    loads[3].wait()
    pl.semaphore_wait(near_sem, 4)

    for k in (4, 3, 5, 2, 6, 1, 7):
        remote(
            tok.at[x, y], tok.at[x, y], t1_send.at[k - 1], t1_recv.at[k - 1], at_y(k)
        )

    def tok_first_wait():
        for k in range(1, n):
            ref = tok.at[x, (y + n - k) % n]
            copy_of(
                ref, ref, t1_send.at[k - 1], t1_recv.at[k - 1], sibling
            ).wait_recv()

    def tok_send_on(held, via, lo=0, hi=N):
        delta = (held + via) % n
        ref = tok.at[(x + held + n) % n, lo:hi]
        at = SLOT[delta] if (lo, hi) != (n // 2, n) else 0
        remote(ref, ref, t2_send.at[at], t2_recv.at[at], at_x(-via))

    def tok_wait(delta, lo=0, hi=N):
        ref = tok.at[(x + delta + n) % n, lo:hi]
        at = SLOT[delta % n] if (lo, hi) != (n // 2, n) else 0
        copy_of(ref, ref, t2_send.at[at], t2_recv.at[at], sibling).wait_recv()

    def tok_relay():
        for side in (2, -2):
            tok_wait(side)
            tok_send_on(side, side, *((0, n // 2) if side == 2 else (n // 2, n)))
            tok_send_on(side, side // 2)

    def multiply(index):
        lo, hi = GROUPS[index]
        block = 2 * rows
        m = (hi - lo) * block
        dims = (((1,), (1,)), ((), ()))
        total = lax.dot_general(
            gu[0, lo:hi].reshape(m, gu.shape[-1]), wg[...], dims,
            preferred_element_type=F32,
        )
        total += lax.dot_general(
            gu[1, lo:hi].reshape(m, gu.shape[-1]), wu[...], dims,
            preferred_element_type=F32,
        )
        for i in range(hi - lo):
            parts[index][:, i] = (
                total[i * block:(i + 1) * block]
                .reshape(n, block // n, total.shape[-1]).astype(BF16)
            )
        for k in (4, 3, 5, 2, 6, 1, 7):
            remote(
                parts[index].at[(y + k) % n], recvs[index].at[k - 1],
                s1_send.at[index, k - 1], s1_recv.at[index, k - 1], at_y(k),
            )

    def reduce_first(index):
        lo, hi = GROUPS[index]
        for k in range(1, n):
            ref = recvs[index].at[k - 1]
            copy_of(
                ref, ref, s1_send.at[index, k - 1], s1_recv.at[index, k - 1], sibling
            ).wait_recv()
        total = parts[index][y].astype(F32)
        for k in range(1, n):
            total += recvs[index][k - 1].astype(F32)
        sums[lo:hi] = total.astype(BF16)
        for slot in range(lo, hi):
            owner = (z + ORDER[slot]) % n

            @pl.when(owner == x)
            def _():
                pltpu.make_async_copy(
                    sums.at[slot], part2.at[x], s2_recv.at[x]
                ).start()

            @pl.when(owner != x)
            def _():
                copy_of(
                    sums.at[slot], part2.at[x], s2_send.at[slot], s2_recv.at[x],
                    (gx, owner * n + y),
                ).start()

    def weights(chunk, result, to, sem):
        right = gu[chunk].reshape(n * 2 * rows, gu.shape[-1])
        result[...] = lax.dot_general(
            tok2[...], right, (((0,), (0,)), ((), ())), preferred_element_type=F32
        ).astype(BF16)
        store = pltpu.make_async_copy(result, to, sem)
        store.start()
        return store

    loads[4].wait()
    loads[5].wait()
    for chunk in range(2):
        sib_wait(0, chunk)
    multiply(0)

    for chunk in range(2):
        for side in (2, -2):
            z_wait(side, chunk)
            if (chunk == 0) == (side == 2):
                z_send_on(side, side, chunk)
            z_send_on(side, side // 2, chunk)
            sib_share(side, chunk)
    for chunk in range(2):
        for side in (2, -2):
            sib_wait(side, chunk)
    multiply(1)

    tok_first_wait()
    for via in (2, -2, 1, -1):
        tok_send_on(0, via)

    for chunk in range(2):
        for side in (1, -1):
            z_wait(side, chunk)
            sib_share(side, chunk)
    for chunk in range(2):
        for side in (1, -1):
            sib_wait(side, chunk)
    multiply(2)

    reduce_first(0)

    for chunk in range(2):
        for side in (3, -3):
            z_wait(side, chunk)
            sib_share(side, chunk)
        z_wait(4, chunk)
        sib_share(4, chunk)
    tok_relay()
    for chunk in range(2):
        for side in (3, -3, 4):
            sib_wait(side, chunk)
    multiply(3)
    reduce_first(1)
    reduce_first(2)

    for side in (1, -1, 3, -3):
        tok_wait(side)
    tok_wait(4, 0, n // 2)
    tok_wait(4, n // 2, n)

    per = tok.shape[2]
    for slot in range(n):
        block = (z + ORDER[slot]) % n
        for pair in range(n // 2):
            two = tok[block, 2 * pair:2 * pair + 2].astype(F32)
            start = (slot * n + 2 * pair) * per
            tok2[start:start + 2 * per] = (
                two.reshape(2 * per, tok.shape[-1]).astype(BF16)
            )
    store_g = weights(0, dwg, dwg_hbm, store_sem.at[0])
    store_u = weights(1, dwu, dwu_hbm, store_sem.at[1])
    reduce_first(3)

    for copy in pending:
        copy.wait_send()
    store_g.wait()
    store_u.wait()
    for j in range(n):
        pltpu.make_async_copy(sums.at[0], part2.at[j], s2_recv.at[j]).wait()
    total = part2[0].astype(F32)
    for j in range(1, n):
        total += part2[j].astype(F32)
    out_ref[...] = total.astype(BF16)
    for slot in range(n):
        @pl.when((z + ORDER[slot]) % n != x)
        def _():
            copy_of(
                sums.at[slot], part2.at[0], s2_send.at[slot], s2_recv.at[0], sibling
            ).wait_send()


def solution(mesh):
    def local(tokens, gate_pre, up_pre, hidden_grad, w_gate, w_up):
        per, d = tokens.shape
        rows, ff = gate_pre.shape
        n = N
        ng = len(GROUPS)
        hbm = pl.BlockSpec(memory_space=pltpu.HBM)
        anywhere = pl.BlockSpec(memory_space=pl.ANY)
        dma = pltpu.SemaphoreType.DMA
        scratch = [
            pltpu.VMEM((rows, ff), BF16),
            pltpu.VMEM((rows, ff), BF16),
            pltpu.VMEM((rows, ff), BF16),
            pltpu.VMEM((d, ff), BF16),
            pltpu.VMEM((d, ff), BF16),
            pltpu.VMEM((2, n, 2, rows, ff), BF16),
            pltpu.VMEM((n, n, per, d), BF16),
            pltpu.VMEM((n * n * per, d), BF16),
            pltpu.VMEM((d, ff), BF16),
            pltpu.VMEM((d, ff), BF16),
            pltpu.VMEM((n, per, d), BF16),
            pltpu.VMEM((n, per, d), BF16),
        ]
        scratch += [pltpu.VMEM((n, hi - lo, per, d), BF16) for lo, hi in GROUPS]
        scratch += [pltpu.VMEM((n - 1, hi - lo, per, d), BF16) for lo, hi in GROUPS]
        scratch += [
            dma((6,)), dma((2,)),
            dma((n, 2)), dma((n, 2)),
            dma((n, 2)), dma((n, 2)),
            dma((n - 1,)), dma((n - 1,)),
            dma((n,)), dma((n,)),
            dma((ng, n - 1)), dma((ng, n - 1)),
            dma((n,)), dma((n,)),
            pltpu.SemaphoreType.REGULAR,
        ]
        return pl.pallas_call(
            functools.partial(kernel, rows),
            out_shape=(
                jax.ShapeDtypeStruct((per, d), BF16),
                jax.ShapeDtypeStruct((d, ff), BF16),
                jax.ShapeDtypeStruct((d, ff), BF16),
            ),
            in_specs=[hbm] * 6,
            out_specs=(pl.BlockSpec(memory_space=pltpu.VMEM), anywhere, anywhere),
            scratch_shapes=scratch,
            compiler_params=pltpu.CompilerParams(
                collective_id=0, has_side_effects=True,
                vmem_limit_bytes=VMEM_MIB * 1024 * 1024,
            ),
            cost_estimate=pl.CostEstimate(
                flops=8 * n * n * per * d * ff, bytes_accessed=8 * d * ff,
                transcendentals=rows * ff,
            ),
        )(tokens, gate_pre, up_pre, hidden_grad, w_gate, w_up)

    return jax.shard_map(
        local,
        mesh=mesh,
        in_specs=(
            P("gy", "gx"),
            P("gx", "gy"),
            P("gx", "gy"),
            P("gx", "gy"),
            P("gx", "gy"),
            P("gx", "gy"),
        ),
        out_specs=(P("gy", "gx"), P("gx", "gy"), P("gx", "gy")),
        check_vma=False,
    )
```

time: 400 us -> 54.6 us (0.14)
  the two profiles are of different devices: /device:TPU:2 before, /device:TPU:10 now
where the time goes in v2:
time: 54.6 us; the launch traced here: 54.4 us
  Pallas kernels  49.4 us (90%)
  local copies, waits for them, and re-layouts  4.38 us (8%)
  between operations  0.64 us (1%)
    pallas_call x1, Pallas kernels, local(): pl.pallas_call(functools.partial(kernel, rows), out_shape=(jax.ShapeDtype...  49.4 us
    unnamed x5, local copies, waits for them, and re-layouts  4.38 us

profile of v2, /device:TPU:10, one launch (start us, length us, event | category | flops | bytes accessed | tf_op | source)
XLA Modules:
  0.0 54.4 jit_solution(15650813829431410317)
XLA Ops:
  0.6 49.4 %shard_map.85 = (bf16[8,640]{1,0:T(8,128)(2,1)}, bf16[640,640]{1,0:T(8,128)(2,1)}, bf16[640,640]{1,0:T(8,128)(2,1)}) custom-call(bf16[8,640]{1,0:T(8,128)(2,1)} %refs_0_.1, bf16[32,640]{1,0:T(8,128)(2,1)} %refs_1_.1, bf16[32,640]{1,0:T(8,128)(2,1)} %refs_2_.1, bf16[32,640]{1,0:T(8,128)(2,1)} %refs_3_.1, bf16[640,640]{1,0:T(8,128)(2,1)} %refs_4_.1, ...), custom_call_target="tpu_custom_call" | custom-call | flops 1677721600 | bytes 3276800 | tf_op jit(solution)/shard_map/pallas_call | solution.py:351
  50.0 1.3 %copy.12 = bf16[8,640]{1,0:T(8,128)(2,1)} copy(bf16[8,640]{1,0:T(8,128)(2,1)} %get-tuple-element.6) | data formatting | bytes 20480
  51.3 0.0 copy-start
  51.3 2.2 %copy.13 = bf16[640,640]{1,0:T(8,128)(2,1)} copy(bf16[640,640]{1,0:T(8,128)(2,1)} %get-tuple-element.7) | data formatting | bytes 1638400
  53.5 0.0 copy-done
  53.5 0.9 %copy.14 = bf16[640,640]{1,0:T(8,128)(2,1)} copy(bf16[640,640]{1,0:T(8,128)(2,1)S(1)} %copy-done) | data formatting | bytes 1638400
Async XLA Ops:
  51.3 2.2 %copy-start = (bf16[640,640]{1,0:T(8,128)(2,1)S(1)}, bf16[640,640]{1,0:T(8,128)(2,1)}, u32[]{:S(2)}) copy-start(bf16[640,640]{1,0:T(8,128)(2,1)} %get-tuple-element.8) | copy-start | bytes 2457604

commit v3 on v2

--- a/solution.py
+++ b/solution.py
@@ -13,9 +13,8 @@
 VMEM_MIB = 60
 
 
-ORDER = (0, 2, 6, 1, 7, 3, 5, 4)
-SLOT = {delta: slot for slot, delta in enumerate(ORDER)}
-GROUPS = ((0, 1), (1, 3), (3, 5), (5, 8))
+GROUPS = ((0, 3), (3, 5), (5, 7), (7, 8))
+AHEAD = 3
 N = 8
 
 
@@ -33,15 +32,15 @@
     (
         load_sem, store_sem, z_send, z_recv, sib_send, sib_recv,
         t1_send, t1_recv, t2_send, t2_recv, s1_send, s1_recv, s2_send, s2_recv,
-        near_sem,
+        near_sem, up_sem,
     ) = more[2 * ng:]
     gx = lax.axis_index("gx")
     gy = lax.axis_index("gy")
     z, c = gx // 2, gx % 2
     x, y = gy // n, gy % n
 
-    def at_z(step):
-        return (((z + step + n) % n) * 2 + c, gy)
+    def at_z(chip):
+        return (chip * 2 + c, gy)
 
     def at_x(step):
         return (gx, ((x + step + n) % n) * n + y)
@@ -81,8 +80,10 @@
 
     barrier = pltpu.get_barrier_semaphore()
     near = (1, -1, 2, -2)
-    for step in near:
-        signal(barrier, at_z(step))
+    for chip in range(1, n):
+        @pl.when(chip > z)
+        def _():
+            signal(barrier, at_z(chip))
     signal(barrier, sibling)
     for step in near:
         signal(barrier, at_x(step))
@@ -94,46 +95,33 @@
     up = up_v[...].astype(F32)
     grad = grad_v[...].astype(F32)
     sig = 1.0 / (1.0 + jnp.exp(-gate))
-    gu[0, 0, c] = (grad * up * sig * (1.0 + gate * (1.0 - sig))).astype(BF16)
-    gu[1, 0, c] = (grad * gate * sig).astype(BF16)
-
-    pl.semaphore_wait(barrier, 13)
-
-    def z_send_on(held, via, chunk):
-        delta = (held + via) % n
-        remote(
-            gu.at[chunk, SLOT[held % n], c], gu.at[chunk, SLOT[delta], c],
-            z_send.at[SLOT[delta], chunk], z_recv.at[SLOT[delta], chunk],
-            at_z(-via),
-        )
-
-    def z_wait(delta, chunk):
-        ref = gu.at[chunk, SLOT[delta % n], c]
-        copy_of(
-            ref, ref, z_send.at[SLOT[delta % n], chunk],
-            z_recv.at[SLOT[delta % n], chunk], sibling,
-        ).wait_recv()
-
-    def sib_share(delta, chunk):
-        slot = SLOT[delta % n]
-        ref = gu.at[chunk, slot, c]
-        remote(ref, ref, sib_send.at[slot, chunk], sib_recv.at[slot, chunk], sibling)
-
-    def sib_wait(delta, chunk):
-        slot = SLOT[delta % n]
-        ref = gu.at[chunk, slot, 1 - c]
-        copy_of(
-            ref, ref, sib_send.at[slot, chunk], sib_recv.at[slot, chunk], sibling
-        ).wait_recv()
-
-    for chunk in range(2):
-        for via in (2, -2):
-            z_send_on(0, via, chunk)
-    for chunk in range(2):
-        sib_share(0, chunk)
-    for chunk in range(2):
-        for via in (1, -1):
-            z_send_on(0, via, chunk)
+    gu[0, z, c] = (grad * up * sig * (1.0 + gate * (1.0 - sig))).astype(BF16)
+    gu[1, z, c] = (grad * gate * sig).astype(BF16)
+
+    pl.semaphore_wait(barrier, z + 9)
+
+    def z_copy(chip):
+        own = gu.at[:, z, c]
+        return copy_of(own, own, z_send.at[chip], z_recv.at[z], at_z(chip))
+
+    def z_arrive(chip):
+        ref = gu.at[:, chip, c]
+        copy_of(ref, ref, z_send.at[chip], z_recv.at[chip], sibling).wait_recv()
+
+    def share(chip, half):
+        ref = gu.at[:, chip, half]
+        return copy_of(ref, ref, sib_send.at[chip], sib_recv.at[chip], sibling)
+
+    share(z, c).start()
+    for chip in range(n - 1):
+        @pl.when(chip < z)
+        def _():
+            signal(up_sem.at[z], at_z(chip))
+            z_copy(chip).start()
+
+    def send_up(chip):
+        pl.semaphore_wait(up_sem.at[chip], 1)
+        z_copy(chip).start()
 
     for step in (2, -2):
         signal(near_sem, at_x(step))
@@ -156,12 +144,12 @@
     def tok_send_on(held, via, lo=0, hi=N):
         delta = (held + via) % n
         ref = tok.at[(x + held + n) % n, lo:hi]
-        at = SLOT[delta] if (lo, hi) != (n // 2, n) else 0
+        at = delta if (lo, hi) != (n // 2, n) else 0
         remote(ref, ref, t2_send.at[at], t2_recv.at[at], at_x(-via))
 
     def tok_wait(delta, lo=0, hi=N):
         ref = tok.at[(x + delta + n) % n, lo:hi]
-        at = SLOT[delta % n] if (lo, hi) != (n // 2, n) else 0
+        at = delta % n if (lo, hi) != (n // 2, n) else 0
         copy_of(ref, ref, t2_send.at[at], t2_recv.at[at], sibling).wait_recv()
 
     def tok_relay():
@@ -205,20 +193,18 @@
         for k in range(1, n):
             total += recvs[index][k - 1].astype(F32)
         sums[lo:hi] = total.astype(BF16)
-        for slot in range(lo, hi):
-            owner = (z + ORDER[slot]) % n
-
-            @pl.when(owner == x)
+        for chip in range(lo, hi):
+            @pl.when(x == chip)
             def _():
                 pltpu.make_async_copy(
-                    sums.at[slot], part2.at[x], s2_recv.at[x]
+                    sums.at[chip], part2.at[x], s2_recv.at[x]
                 ).start()
 
-            @pl.when(owner != x)
+            @pl.when(x != chip)
             def _():
                 copy_of(
-                    sums.at[slot], part2.at[x], s2_send.at[slot], s2_recv.at[x],
-                    (gx, owner * n + y),
+                    sums.at[chip], part2.at[x], s2_send.at[chip], s2_recv.at[x],
+                    (gx, chip * n + y),
                 ).start()
 
     def weights(chunk, result, to, sem):
@@ -232,50 +218,32 @@
 
     loads[4].wait()
     loads[5].wait()
-    for chunk in range(2):
-        sib_wait(0, chunk)
-    multiply(0)
-
-    for chunk in range(2):
-        for side in (2, -2):
-            z_wait(side, chunk)
-            if (chunk == 0) == (side == 2):
-                z_send_on(side, side, chunk)
-            z_send_on(side, side // 2, chunk)
-            sib_share(side, chunk)
-    for chunk in range(2):
-        for side in (2, -2):
-            sib_wait(side, chunk)
-    multiply(1)
-
-    tok_first_wait()
-    for via in (2, -2, 1, -1):
-        tok_send_on(0, via)
-
-    for chunk in range(2):
-        for side in (1, -1):
-            z_wait(side, chunk)
-            sib_share(side, chunk)
-    for chunk in range(2):
-        for side in (1, -1):
-            sib_wait(side, chunk)
-    multiply(2)
-
-    reduce_first(0)
-
-    for chunk in range(2):
-        for side in (3, -3):
-            z_wait(side, chunk)
-            sib_share(side, chunk)
-        z_wait(4, chunk)
-        sib_share(4, chunk)
+    for chip in range(1, n):
+        @pl.when((chip > z) & (chip <= z + AHEAD))
+        def _():
+            send_up(chip)
+
+    for index, (lo, hi) in enumerate(GROUPS):
+        for chip in range(lo, hi):
+            if AHEAD < chip + AHEAD < n:
+                @pl.when(chip > z)
+                def _():
+                    send_up(chip + AHEAD)
+
+            @pl.when(chip != z)
+            def _():
+                z_arrive(chip)
+                share(chip, c).start()
+        for chip in range(lo, hi):
+            share(chip, 1 - c).wait_recv()
+        multiply(index)
+        if index == 0:
+            tok_first_wait()
+            for via in (2, -2, 1, -1):
+                tok_send_on(0, via)
     tok_relay()
-    for chunk in range(2):
-        for side in (3, -3, 4):
-            sib_wait(side, chunk)
-    multiply(3)
-    reduce_first(1)
-    reduce_first(2)
+    for index in range(ng - 1):
+        reduce_first(index)
 
     for side in (1, -1, 3, -3):
         tok_wait(side)
@@ -283,17 +251,16 @@
     tok_wait(4, n // 2, n)
 
     per = tok.shape[2]
-    for slot in range(n):
-        block = (z + ORDER[slot]) % n
+    for chip in range(n):
         for pair in range(n // 2):
-            two = tok[block, 2 * pair:2 * pair + 2].astype(F32)
-            start = (slot * n + 2 * pair) * per
+            two = tok[chip, 2 * pair:2 * pair + 2].astype(F32)
+            start = (chip * n + 2 * pair) * per
             tok2[start:start + 2 * per] = (
                 two.reshape(2 * per, tok.shape[-1]).astype(BF16)
             )
     store_g = weights(0, dwg, dwg_hbm, store_sem.at[0])
     store_u = weights(1, dwu, dwu_hbm, store_sem.at[1])
-    reduce_first(3)
+    reduce_first(ng - 1)
 
     for copy in pending:
         copy.wait_send()
@@ -305,11 +272,17 @@
     for j in range(1, n):
         total += part2[j].astype(F32)
     out_ref[...] = total.astype(BF16)
-    for slot in range(n):
-        @pl.when((z + ORDER[slot]) % n != x)
+    for chip in range(n):
+        share(chip, c).wait_send()
+
+        @pl.when(chip != z)
+        def _():
+            z_copy(chip).wait_send()
+
+        @pl.when(chip != x)
         def _():
             copy_of(
-                sums.at[slot], part2.at[0], s2_send.at[slot], s2_recv.at[0], sibling
+                sums.at[chip], part2.at[0], s2_send.at[chip], s2_recv.at[0], sibling
             ).wait_send()
 
 
@@ -340,13 +313,13 @@
         scratch += [pltpu.VMEM((n - 1, hi - lo, per, d), BF16) for lo, hi in GROUPS]
         scratch += [
             dma((6,)), dma((2,)),
-            dma((n, 2)), dma((n, 2)),
-            dma((n, 2)), dma((n, 2)),
+            dma((n,)), dma((n,)),
+            dma((n,)), dma((n,)),
             dma((n - 1,)), dma((n - 1,)),
             dma((n,)), dma((n,)),
             dma((ng, n - 1)), dma((ng, n - 1)),
             dma((n,)), dma((n,)),
-            pltpu.SemaphoreType.REGULAR,
+            pltpu.SemaphoreType.REGULAR, pltpu.SemaphoreType.REGULAR((n,)),
         ]
         return pl.pallas_call(
             functools.partial(kernel, rows),

time: 54.6 us -> 54 us (0.989)
  the two profiles are of different devices: /device:TPU:10 before, /device:TPU:910 now
where the time goes in v3:
time: 54 us; the launch traced here: 53.8 us
  Pallas kernels  48.8 us (90%)
  local copies, waits for them, and re-layouts  4.38 us (8%)
  between operations  0.64 us (1%)
    pallas_call x1, Pallas kernels, local(): pl.pallas_call(functools.partial(kernel, rows), out_shape=(jax.ShapeDtype...  48.8 us
    unnamed x5, local copies, waits for them, and re-layouts  4.38 us

profile of v3, /device:TPU:910, one launch (start us, length us, event | category | flops | bytes accessed | tf_op | source)
XLA Modules:
  0.0 53.8 jit_solution(9110362455278801884)
XLA Ops:
  0.6 48.8 %shard_map.85 = (bf16[8,640]{1,0:T(8,128)(2,1)}, bf16[640,640]{1,0:T(8,128)(2,1)}, bf16[640,640]{1,0:T(8,128)(2,1)}) custom-call(bf16[8,640]{1,0:T(8,128)(2,1)} %refs_0_.1, bf16[32,640]{1,0:T(8,128)(2,1)} %refs_1_.1, bf16[32,640]{1,0:T(8,128)(2,1)} %refs_2_.1, bf16[32,640]{1,0:T(8,128)(2,1)} %refs_3_.1, bf16[640,640]{1,0:T(8,128)(2,1)} %refs_4_.1, ...), custom_call_target="tpu_custom_call" | custom-call | flops 1677721600 | bytes 3276800 | tf_op jit(solution)/shard_map/pallas_call | solution.py:324
  49.4 1.3 %copy.12 = bf16[8,640]{1,0:T(8,128)(2,1)} copy(bf16[8,640]{1,0:T(8,128)(2,1)} %get-tuple-element.6) | data formatting | bytes 20480
  50.7 0.0 copy-start
  50.7 2.2 %copy.13 = bf16[640,640]{1,0:T(8,128)(2,1)} copy(bf16[640,640]{1,0:T(8,128)(2,1)} %get-tuple-element.7) | data formatting | bytes 1638400
  52.9 0.0 copy-done
  52.9 0.9 %copy.14 = bf16[640,640]{1,0:T(8,128)(2,1)} copy(bf16[640,640]{1,0:T(8,128)(2,1)S(1)} %copy-done) | data formatting | bytes 1638400
Async XLA Ops:
  50.7 2.2 %copy-start = (bf16[640,640]{1,0:T(8,128)(2,1)S(1)}, bf16[640,640]{1,0:T(8,128)(2,1)}, u32[]{:S(2)}) copy-start(bf16[640,640]{1,0:T(8,128)(2,1)} %get-tuple-element.8) | copy-start | bytes 2457604

commit v4 on v3

--- a/solution.py
+++ b/solution.py
@@ -223,6 +223,10 @@
         def _():
             send_up(chip)
 
+    tok_first_wait()
+    for via in (2, -2, 1, -1):
+        tok_send_on(0, via)
+
     for index, (lo, hi) in enumerate(GROUPS):
         for chip in range(lo, hi):
             if AHEAD < chip + AHEAD < n:
@@ -238,10 +242,7 @@
             share(chip, 1 - c).wait_recv()
         multiply(index)
         if index == 0:
-            tok_first_wait()
-            for via in (2, -2, 1, -1):
-                tok_send_on(0, via)
-    tok_relay()
+            tok_relay()
     for index in range(ng - 1):
         reduce_first(index)
 

time: 54 us -> 53.4 us (0.989)
  Pallas kernels: 48.8 us -> 48 us
    pallas_call x1, Pallas kernels: 48.8 us -> 48 us  [local(): pl.pallas_call(functools.partial(kernel, rows), out_shape=(jax.ShapeDtype...]
where the time goes in v4:
time: 53.4 us; the launch traced here: 53 us
  Pallas kernels  48 us (90%)
  local copies, waits for them, and re-layouts  4.38 us (8%)
  between operations  0.64 us (1%)
    pallas_call x1, Pallas kernels, local(): pl.pallas_call(functools.partial(kernel, rows), out_shape=(jax.ShapeDtype...  48 us
    unnamed x5, local copies, waits for them, and re-layouts  4.38 us

profile of v4, /device:TPU:910, one launch (start us, length us, event | category | flops | bytes accessed | tf_op | source)
XLA Modules:
  0.0 53.0 jit_solution(10534911731491668418)
XLA Ops:
  0.6 48.0 %shard_map.85 = (bf16[8,640]{1,0:T(8,128)(2,1)}, bf16[640,640]{1,0:T(8,128)(2,1)}, bf16[640,640]{1,0:T(8,128)(2,1)}) custom-call(bf16[8,640]{1,0:T(8,128)(2,1)} %refs_0_.1, bf16[32,640]{1,0:T(8,128)(2,1)} %refs_1_.1, bf16[32,640]{1,0:T(8,128)(2,1)} %refs_2_.1, bf16[32,640]{1,0:T(8,128)(2,1)} %refs_3_.1, bf16[640,640]{1,0:T(8,128)(2,1)} %refs_4_.1, ...), custom_call_target="tpu_custom_call" | custom-call | flops 1677721600 | bytes 3276800 | tf_op jit(solution)/shard_map/pallas_call | solution.py:325
  48.7 1.3 %copy.12 = bf16[8,640]{1,0:T(8,128)(2,1)} copy(bf16[8,640]{1,0:T(8,128)(2,1)} %get-tuple-element.6) | data formatting | bytes 20480
  50.0 0.0 copy-start
  50.0 2.2 %copy.13 = bf16[640,640]{1,0:T(8,128)(2,1)} copy(bf16[640,640]{1,0:T(8,128)(2,1)} %get-tuple-element.7) | data formatting | bytes 1638400
  52.2 0.0 copy-done
  52.2 0.9 %copy.14 = bf16[640,640]{1,0:T(8,128)(2,1)} copy(bf16[640,640]{1,0:T(8,128)(2,1)S(1)} %copy-done) | data formatting | bytes 1638400
Async XLA Ops:
  50.0 2.2 %copy-start = (bf16[640,640]{1,0:T(8,128)(2,1)S(1)}, bf16[640,640]{1,0:T(8,128)(2,1)}, u32[]{:S(2)}) copy-start(bf16[640,640]{1,0:T(8,128)(2,1)} %get-tuple-element.8) | copy-start | bytes 2457604
